TPU v7x, 32 devices: a whole 2x2x4 slice. The times are simulated.
32 devices in a mesh: dp: 8 (over z, y), mp: 4 (over x, core).
Axes of the slice: x: 2, y: 2, z: 4, core: 2. Of those that a mesh axis runs over, the one named last changes fastest.
Arguments:
- image_emb: bfloat16 [6144, 1152], P(('dp', 'mp')), may hold values from -0.1875 to 0.1875
- text_emb: bfloat16 [6144, 1152], P(('dp', 'mp')), may hold values from -0.1875 to 0.1875
- log_scale: float32 [1], replicated, may hold values from 1.6 to 3
- bias: float32 [1], replicated, may hold values from -4 to -1
Outputs:
- image_grad: float32 [6144, 1152], P(('dp', 'mp'))
- text_grad: float32 [6144, 1152], P(('dp', 'mp'))
All inputs are finite; a program needn't handle non-finite values.
Results may differ from a plain program's by a relative error of at most 0.0033.
Values may be sent and summed in bfloat16 or wider, within the bound.
A program may use at most 64 MiB of HBM per device.

v0:
```python
import jax
import jax.numpy as jnp
from jax import lax
from jax.sharding import PartitionSpec as P

SHIFTS = 4


def shifted(value, axis, steps):
    count = lax.axis_size(axis)
    pairs = [(source, (source + steps) % count) for source in range(count)]
    return lax.ppermute(value, axis, pairs)


def loss_weights(logits, scale, is_own):
    row_ids = lax.broadcasted_iota(jnp.int32, logits.shape, 0)
    col_ids = lax.broadcasted_iota(jnp.int32, logits.shape, 1)
    target = jnp.where(jnp.logical_and(row_ids == col_ids, is_own), 1.0, 0.0).astype(jnp.float32)
    return (scale * (jax.nn.sigmoid(logits) - target)).astype(jnp.bfloat16)


def local(image_emb, text_emb, log_scale, bias):
    scale = jnp.exp(log_scale[0])
    offset = bias[0]
    text_block = text_emb
    image_grad = jnp.zeros(image_emb.shape, jnp.float32)
    running = jnp.zeros(text_emb.shape, jnp.float32)
    for step in range(SHIFTS + 1):
        if step > 0:
            text_block = shifted(text_block, ("dp", "mp"), 1)
            running = shifted(running, ("dp", "mp"), 1)
        inner = lax.dot_general(
            image_emb, text_block, (((1,), (1,)), ((), ())), preferred_element_type=jnp.float32
        )
        weights = loss_weights(scale * inner + offset, scale, step == 0)
        image_grad = image_grad + jnp.dot(weights, text_block, preferred_element_type=jnp.float32)
        term = lax.dot_general(
            weights, image_emb, (((0,), (0,)), ((), ())), preferred_element_type=jnp.float32
        )
        running = running + term
    text_grad = shifted(running, ("dp", "mp"), -SHIFTS)
    return (image_grad, text_grad)


def solution(mesh):
    return jax.shard_map(
        local,
        mesh=mesh,
        in_specs=(P(("dp", "mp"), None), P(("dp", "mp"), None), P(), P()),
        out_specs=(P(("dp", "mp"), None), P(("dp", "mp"), None)),
        check_vma=False,
    )
```

profile of v0, /device:TPU:0, one launch (start us, length us, event | category | flops | bytes accessed | tf_op | source)
XLA Modules:
  0.0 98.7 jit_solution(14082402780142602468)
XLA Ops:
  0.6 0.0 copy-start
  2.0 0.0 copy-done
  2.0 1.4 %fusion.31 = bf16[192,192]{1,0:T(8,128)(2,1)S(1)} fusion(bf16[192,1152]{1,0:T(8,128)(2,1)S(1)} %copy-done, bf16[192,1152]{1,0:T(8,128)(2,1)} %param.5, f32[]{:T(128)} %bitcast.32, f32[]{:T(128)} %bitcast), kind=kOutput, calls=%fused_computation.41 | convolution fusion | flops 85303296 | bytes 958472 | tf_op jit(solution)/shard_map/dot_general | solution.py:32
  3.4 0.0 copy-start.1
  3.4 0.3 fusion.37
  3.7 0.5 collective-permute-start.4
  4.2 0.2 copy-done.1
  4.4 2.4 %collective-permute-start = (bf16[192,1152]{1,0:T(8,128)(2,1)S(1)}, bf16[192,1152]{1,0:T(8,128)(2,1)S(1)}, u32[]{:S(2)}, u32[]{:S(2)}) collective-permute-start(bf16[192,1152]{1,0:T(8,128)(2,1)S(1)} %copy-done.1), channel_id=1, source_target_pairs={{0,1},{1,2},{2,3},{3,4},{4,5},{5,6},{6,7},{7,8},{8,9},{9,10},{10,1... | collective-permute-start | bytes 1327112 | tf_op jit(solution)/shard_map/ppermute | solution.py:12
  6.9 18.8 %collective-permute-done = bf16[192,1152]{1,0:T(8,128)(2,1)S(1)} collective-permute-done((bf16[192,1152]{1,0:T(8,128)(2,1)S(1)}, bf16[192,1152]{1,0:T(8,128)(2,1)S(1)}, u32[]{:S(2)}, u32[]{:S(2)}) %collective-permute-start) | collective-permute-done | bytes 442400 | tf_op jit(solution)/shard_map/ppermute | solution.py:12
  25.6 0.0 collective-permute-start.1
  25.6 0.3 fusion.32
  26.0 0.0 collective-permute-done.4
  26.0 0.3 convolution_add_fusion
  26.3 0.1 collective-permute-start.5
  26.4 10.6 %collective-permute-done.1 = bf16[192,1152]{1,0:T(8,128)(2,1)S(1)} collective-permute-done((bf16[192,1152]{1,0:T(8,128)(2,1)S(1)}, bf16[192,1152]{1,0:T(8,128)(2,1)S(1)}, u32[]{:S(2)}, u32[]{:S(2)}) %collective-permute-start.1) | collective-permute-done | bytes 442400 | tf_op jit(solution)/shard_map/ppermute | solution.py:12
  37.0 0.0 collective-permute-start.2
  37.0 0.3 fusion.33
  37.3 0.3 fusion.38
  37.7 8.8 %collective-permute-done.5 = f32[192,1152]{1,0:T(8,128)S(1)} collective-permute-done((f32[192,1152]{1,0:T(8,128)S(1)}, f32[192,1152]{1,0:T(8,128)S(1)}, u32[]{:S(2)}, u32[]{:S(2)}) %collective-permute-start.5) | collective-permute-done | bytes 884768 | tf_op jit(solution)/shard_map/ppermute | solution.py:12
  46.4 0.1 add.77
  46.5 0.1 collective-permute-start.6
  46.6 4.6 %collective-permute-done.2 = bf16[192,1152]{1,0:T(8,128)(2,1)S(1)} collective-permute-done((bf16[192,1152]{1,0:T(8,128)(2,1)S(1)}, bf16[192,1152]{1,0:T(8,128)(2,1)S(1)}, u32[]{:S(2)}, u32[]{:S(2)}) %collective-permute-start.2) | collective-permute-done | bytes 442400 | tf_op jit(solution)/shard_map/ppermute | solution.py:12
  51.2 0.0 collective-permute-start.3
  51.2 0.3 fusion.34
  51.5 0.3 fusion.39
  51.9 10.8 %collective-permute-done.6 = f32[192,1152]{1,0:T(8,128)S(1)} collective-permute-done((f32[192,1152]{1,0:T(8,128)S(1)}, f32[192,1152]{1,0:T(8,128)S(1)}, u32[]{:S(2)}, u32[]{:S(2)}) %collective-permute-start.6) | collective-permute-done | bytes 884768 | tf_op jit(solution)/shard_map/ppermute | solution.py:12
  62.7 0.1 add.78
  62.8 0.1 collective-permute-start.7
  62.8 0.3 fusion.36
  63.1 4.3 %collective-permute-done.3 = bf16[192,1152]{1,0:T(8,128)(2,1)S(1)} collective-permute-done((bf16[192,1152]{1,0:T(8,128)(2,1)S(1)}, bf16[192,1152]{1,0:T(8,128)(2,1)S(1)}, u32[]{:S(2)}, u32[]{:S(2)}) %collective-permute-start.3) | collective-permute-done | bytes 442400 | tf_op jit(solution)/shard_map/ppermute | solution.py:12
  67.4 0.3 fusion.35
  67.8 0.3 fusion.40
  68.1 10.9 %collective-permute-done.7 = f32[192,1152]{1,0:T(8,128)S(1)} collective-permute-done((f32[192,1152]{1,0:T(8,128)S(1)}, f32[192,1152]{1,0:T(8,128)S(1)}, u32[]{:S(2)}, u32[]{:S(2)}) %collective-permute-start.7) | collective-permute-done | bytes 884768 | tf_op jit(solution)/shard_map/ppermute | solution.py:12
  79.0 0.1 add.79
  79.1 0.1 collective-permute-start.8
  79.1 0.3 convolution_add_fusion.4
  79.4 0.3 convolution_add_fusion.3
  79.7 0.3 convolution_add_fusion.2
  80.0 1.2 %convolution_add_fusion.1 = f32[192,1152]{1,0:T(8,128)} fusion(f32[192,1152]{1,0:T(8,128)S(1)} %convolution_add_fusion.2, bf16[192,192]{1,0:T(8,128)(2,1)S(1)} %fusion.35, bf16[192,1152]{1,0:T(8,128)(2,1)S(1)} %collective-permute-done.3), kind=kOutput, calls=%fused_computation.1 | convolution fusion | flops 85155840 | bytes 2285568 | tf_op jit(solution)/shard_map/dot_general | solution.py:36
  81.2 16.6 %collective-permute-done.8 = f32[192,1152]{1,0:T(8,128)S(1)} collective-permute-done((f32[192,1152]{1,0:T(8,128)S(1)}, f32[192,1152]{1,0:T(8,128)S(1)}, u32[]{:S(2)}, u32[]{:S(2)}) %collective-permute-start.8) | collective-permute-done | bytes 884768 | tf_op jit(solution)/shard_map/ppermute | solution.py:12
  97.8 0.9 copy.9
Async XLA Ops:
  0.6 1.4 %copy-start = (bf16[192,1152]{1,0:T(8,128)(2,1)S(1)}, bf16[192,1152]{1,0:T(8,128)(2,1)}, u32[]{:S(2)}) copy-start(bf16[192,1152]{1,0:T(8,128)(2,1)} %param.4) | copy-start | bytes 1327108
  3.4 1.0 %copy-start.1 = (bf16[192,1152]{1,0:T(8,128)(2,1)S(1)}, bf16[192,1152]{1,0:T(8,128)(2,1)}, u32[]{:S(2)}) copy-start(bf16[192,1152]{1,0:T(8,128)(2,1)} %param.5) | copy-start | bytes 1327108
  3.7 22.3 %collective-permute-start.4 = (f32[192,1152]{1,0:T(8,128)S(1)}, f32[192,1152]{1,0:T(8,128)S(1)}, u32[]{:S(2)}, u32[]{:S(2)}) collective-permute-start(f32[192,1152]{1,0:T(8,128)S(1)} %fusion.37), channel_id=1, source_target_pairs={{0,1},{1,2},{2,3},{3,4},{4,5},{5,6},{6,7},{7,8},{8,9},{9,10},{10,1... | collective-permute-start | bytes 2654216 | tf_op jit(solution)/shard_map/ppermute | solution.py:12
  4.4 21.2 %collective-permute-start = (bf16[192,1152]{1,0:T(8,128)(2,1)S(1)}, bf16[192,1152]{1,0:T(8,128)(2,1)S(1)}, u32[]{:S(2)}, u32[]{:S(2)}) collective-permute-start(bf16[192,1152]{1,0:T(8,128)(2,1)S(1)} %copy-done.1), channel_id=1, source_target_pairs={{0,1},{1,2},{2,3},{3,4},{4,5},{5,6},{6,7},{7,8},{8,9},{9,10},{10,1... | collective-permute-start | bytes 1327112 | tf_op jit(solution)/shard_map/ppermute | solution.py:12
  25.6 11.3 %collective-permute-start.1 = (bf16[192,1152]{1,0:T(8,128)(2,1)S(1)}, bf16[192,1152]{1,0:T(8,128)(2,1)S(1)}, u32[]{:S(2)}, u32[]{:S(2)}) collective-permute-start(bf16[192,1152]{1,0:T(8,128)(2,1)S(1)} %collective-permute-done), channel_id=1, source_target_pairs={{0,1},{1,2},{2,3},{3,4},{4,5},{5,6},{6,7},{7,8},{8,9},{9,10},{10,1... | collective-permute-start | bytes 1327112 | tf_op jit(solution)/shard_map/ppermute | solution.py:12
  26.3 20.1 %collective-permute-start.5 = (f32[192,1152]{1,0:T(8,128)S(1)}, f32[192,1152]{1,0:T(8,128)S(1)}, u32[]{:S(2)}, u32[]{:S(2)}) collective-permute-start(f32[192,1152]{1,0:T(8,128)S(1)} %convolution_add_fusion), channel_id=1, source_target_pairs={{0,1},{1,2},{2,3},{3,4},{4,5},{5,6},{6,7},{7,8},{8,9},{9,10},{10,1... | collective-permute-start | bytes 2654216 | tf_op jit(solution)/shard_map/ppermute | solution.py:12
  37.0 14.2 %collective-permute-start.2 = (bf16[192,1152]{1,0:T(8,128)(2,1)S(1)}, bf16[192,1152]{1,0:T(8,128)(2,1)S(1)}, u32[]{:S(2)}, u32[]{:S(2)}) collective-permute-start(bf16[192,1152]{1,0:T(8,128)(2,1)S(1)} %collective-permute-done.1), channel_id=1, source_target_pairs={{0,1},{1,2},{2,3},{3,4},{4,5},{5,6},{6,7},{7,8},{8,9},{9,10},{10,1... | collective-permute-start | bytes 1327112 | tf_op jit(solution)/shard_map/ppermute | solution.py:12
  46.5 16.1 %collective-permute-start.6 = (f32[192,1152]{1,0:T(8,128)S(1)}, f32[192,1152]{1,0:T(8,128)S(1)}, u32[]{:S(2)}, u32[]{:S(2)}) collective-permute-start(f32[192,1152]{1,0:T(8,128)S(1)} %add.77), channel_id=1, source_target_pairs={{0,1},{1,2},{2,3},{3,4},{4,5},{5,6},{6,7},{7,8},{8,9},{9,10},{10,1... | collective-permute-start | bytes 2654216 | tf_op jit(solution)/shard_map/ppermute | solution.py:12
  51.2 16.2 %collective-permute-start.3 = (bf16[192,1152]{1,0:T(8,128)(2,1)S(1)}, bf16[192,1152]{1,0:T(8,128)(2,1)S(1)}, u32[]{:S(2)}, u32[]{:S(2)}) collective-permute-start(bf16[192,1152]{1,0:T(8,128)(2,1)S(1)} %collective-permute-done.2), channel_id=1, source_target_pairs={{0,1},{1,2},{2,3},{3,4},{4,5},{5,6},{6,7},{7,8},{8,9},{9,10},{10,1... | collective-permute-start | bytes 1327112 | tf_op jit(solution)/shard_map/ppermute | solution.py:12
  62.8 16.2 %collective-permute-start.7 = (f32[192,1152]{1,0:T(8,128)S(1)}, f32[192,1152]{1,0:T(8,128)S(1)}, u32[]{:S(2)}, u32[]{:S(2)}) collective-permute-start(f32[192,1152]{1,0:T(8,128)S(1)} %add.78), channel_id=1, source_target_pairs={{0,1},{1,2},{2,3},{3,4},{4,5},{5,6},{6,7},{7,8},{8,9},{9,10},{10,1... | collective-permute-start | bytes 2654216 | tf_op jit(solution)/shard_map/ppermute | solution.py:12
  79.1 18.8 %collective-permute-start.8 = (f32[192,1152]{1,0:T(8,128)S(1)}, f32[192,1152]{1,0:T(8,128)S(1)}, u32[]{:S(2)}, u32[]{:S(2)}) collective-permute-start(f32[192,1152]{1,0:T(8,128)S(1)} %add.79), channel_id=1, source_target_pairs={{0,28},{1,29},{2,30},{3,31},{4,0},{5,1},{6,2},{7,3},{8,4},{9,5},{1... | collective-permute-start | bytes 2654216 | tf_op jit(solution)/shard_map/ppermute | solution.py:12
where the time goes:
time: 99 us; the launch traced here: 98.7 us
  waiting for transfers between devices  85.3 us (86%)
  matrix products  6.68 us (7%)
  starting transfers between devices  3.16 us (3%)
  between operations  2.19 us (2%)
  local copies, waits for them, and re-layouts  1.11 us (1%)
    ppermute x9, waiting for transfers between devices, shifted(): return lax.ppermute(value, axis, pairs)  85.3 us
    ppermute x9, starting transfers between devices, shifted(): return lax.ppermute(value, axis, pairs)  3.16 us
    dot_general x5, matrix products, local(): lax.dot_general(image_emb, text_block, (((1,), (1,)), ((), ())), preferre...  2.76 us
    dot_general x5, matrix products, local(): jnp.dot(weights, text_block, preferred_element_type=jnp.float32)  2.33 us
  transfers between devices with their start and end apart: 9, of which 8 were waited for; matrix products, arithmetic and copies ran while one was open for 5% of the time, Pallas kernels for 0%

commit v1 on v0

v1 whole, which is shorter than its diff:
```python
import jax
import jax.numpy as jnp
from jax import lax
from jax.experimental import pallas as pl
from jax.experimental.pallas import tpu as pltpu
from jax.sharding import PartitionSpec as P

SHIFTS = 4
CHUNKS = 4

FAR = 0
NEAR_OWN, NEAR_FAR = 2, 3
CORE_OWN, CORE_FAR, CORE_NEAR_OWN, CORE_NEAR_FAR = 4, 5, 6, 7


def kernel(log_scale_ref, bias_ref, image_ref, text_ref, image_out, text_out, own, held, total, load_sem, send_sem, recv_sem):
    dp_count, mp_count = lax.axis_size("dp"), lax.axis_size("mp")
    count = dp_count * mp_count
    me = lax.axis_index("dp") * mp_count + lax.axis_index("mp")
    core = lax.rem(me, 2)
    side = lax.rem(me // 2, 2)
    rows = image_ref.shape[0]
    part = rows // CHUNKS

    def place(index):
        return (index // mp_count, lax.rem(index, mp_count))

    after = place(lax.rem(me + SHIFTS, count))
    before = place(lax.rem(me + count - SHIFTS, count))
    near = place(me + 2 - 4 * side)
    twin = place(me + 1 - 2 * core)

    loads = [
        pltpu.make_async_copy(image_ref, own.at[0], load_sem.at[0]),
        pltpu.make_async_copy(text_ref, own.at[1], load_sem.at[1]),
    ]
    for load in loads:
        load.start()

    barrier = pltpu.get_barrier_semaphore()
    for other in (after, before, near, twin):
        pl.semaphore_signal(barrier, inc=1, device_id=other, device_id_type=pl.DeviceIdType.MESH)
    pl.semaphore_wait(barrier, 4)
    for load in loads:
        load.wait()

    def remote(source, slot, chunk, device):
        span = pl.ds(chunk * part, part)
        return pltpu.make_async_remote_copy(
            src_ref=source.at[span],
            dst_ref=held.at[slot, span],
            send_sem=send_sem.at[slot, chunk],
            recv_sem=recv_sem.at[slot, chunk],
            device_id=device,
            device_id_type=pl.DeviceIdType.MESH,
        )

    def far(kind, chunk):
        target = tuple(jnp.where(kind == 0, b, a) for a, b in zip(after, before))
        return remote(own.at[kind], FAR + kind, chunk, target)

    first, second = side, 1 - side
    near_own = [remote(own.at[1 - side], NEAR_OWN, i, near) for i in range(CHUNKS)]
    near_far = [remote(held.at[FAR + side], NEAR_FAR, i, near) for i in range(CHUNKS)]
    core_own = [remote(own.at[1 - core], CORE_OWN, i, twin) for i in range(CHUNKS)]
    core_far = [remote(held.at[FAR + core], CORE_FAR, i, twin) for i in range(CHUNKS)]
    core_near_own = [remote(held.at[NEAR_OWN], CORE_NEAR_OWN, i, twin) for i in range(CHUNKS)]
    core_near_far = [remote(held.at[NEAR_FAR], CORE_NEAR_FAR, i, twin) for i in range(CHUNKS)]
    far_first = [far(first, i) for i in range(CHUNKS)]
    far_second = [far(second, i) for i in range(CHUNKS)]

    for i in range(CHUNKS):
        far_first[i].start()
        near_own[i].start()
    for i in range(CHUNKS):
        far_second[i].start()
        core_own[i].start()

    scale = jnp.exp(jnp.full((1, rows), log_scale_ref[0], jnp.float32))
    offset = bias_ref[0]

    def weights_of(mine, block):
        inner = lax.dot_general(mine, block, (((1,), (1,)), ((), ())), preferred_element_type=jnp.float32)
        return jax.nn.sigmoid(scale * inner + offset)

    def add(slot, kind):
        block = held[slot]
        weights = (scale * weights_of(own[1 - kind], block)).astype(jnp.bfloat16)
        total[1 - kind] += jnp.dot(weights, block, preferred_element_type=jnp.float32)

    row_ids = lax.broadcasted_iota(jnp.int32, (rows, rows), 0)
    col_ids = lax.broadcasted_iota(jnp.int32, (rows, rows), 1)
    target = jnp.where(row_ids == col_ids, 1.0, 0.0).astype(jnp.float32)
    own_weights = (scale * (weights_of(own[0], own[1]) - target)).astype(jnp.bfloat16)
    total[0] = jnp.dot(own_weights, own[1], preferred_element_type=jnp.float32)
    total[1] = lax.dot_general(own_weights, own[0], (((0,), (0,)), ((), ())), preferred_element_type=jnp.float32)

    for copy in core_own:
        copy.wait_recv()
    add(CORE_OWN, core)

    for i in range(CHUNKS):
        far_first[i].wait_recv()
        near_far[i].start()

        @pl.when(side == core)
        def _():
            core_far[i].start()

    add(FAR + first, first)

    for i in range(CHUNKS):
        near_own[i].wait_recv()
        core_near_own[i].start()
    add(NEAR_OWN, side)
    for copy in core_near_own:
        copy.wait_recv()
    add(CORE_NEAR_OWN, side)

    for i in range(CHUNKS):
        far_second[i].wait_recv()

        @pl.when(side != core)
        def _():
            core_far[i].start()

        near_far[i].wait_recv()
        core_near_far[i].start()

    add(FAR + second, second)
    add(NEAR_FAR, 1 - side)
    for copy in core_far:
        copy.wait_recv()
    add(CORE_FAR, 1 - core)
    for copy in core_near_far:
        copy.wait_recv()
    add(CORE_NEAR_FAR, 1 - side)

    stores = [
        pltpu.make_async_copy(total.at[0], image_out, load_sem.at[0]),
        pltpu.make_async_copy(total.at[1], text_out, load_sem.at[1]),
    ]
    for store in stores:
        store.start()
    for copies in (far_first, far_second, near_own, near_far, core_own, core_far, core_near_own, core_near_far):
        for copy in copies:
            copy.wait_send()
    for store in stores:
        store.wait()


def local(image_emb, text_emb, log_scale, bias):
    rows, width = image_emb.shape
    block = jax.ShapeDtypeStruct((rows, width), jnp.float32)
    return pl.pallas_call(
        kernel,
        out_shape=(block, block),
        in_specs=[
            pl.BlockSpec(memory_space=pltpu.SMEM),
            pl.BlockSpec(memory_space=pltpu.SMEM),
            pl.BlockSpec(memory_space=pl.ANY),
            pl.BlockSpec(memory_space=pl.ANY),
        ],
        out_specs=(pl.BlockSpec(memory_space=pl.ANY), pl.BlockSpec(memory_space=pl.ANY)),
        scratch_shapes=[
            pltpu.VMEM((2, rows, width), jnp.bfloat16),
            pltpu.VMEM((8, rows, width), jnp.bfloat16),
            pltpu.VMEM((2, rows, width), jnp.float32),
            pltpu.SemaphoreType.DMA((2,)),
            pltpu.SemaphoreType.DMA((8, CHUNKS)),
            pltpu.SemaphoreType.DMA((8, CHUNKS)),
        ],
        compiler_params=pltpu.CompilerParams(
            collective_id=0, has_side_effects=True, vmem_limit_bytes=32 * 1024 * 1024
        ),
        cost_estimate=pl.CostEstimate(
            flops=20 * 2 * rows * rows * width, bytes_accessed=12 * rows * width, transcendentals=9 * rows * rows
        ),
    )(log_scale, bias, image_emb, text_emb)


def solution(mesh):
    count = 1
    for axis in ("dp", "mp"):
        count *= mesh.shape[axis]
    assert mesh.shape["mp"] % 4 == 0 and count > 2 * SHIFTS
    return jax.shard_map(
        local,
        mesh=mesh,
        in_specs=(P(("dp", "mp"), None), P(("dp", "mp"), None), P(), P()),
        out_specs=(P(("dp", "mp"), None), P(("dp", "mp"), None)),
        check_vma=False,
    )
```

time: 99 us -> 37.9 us (0.38)
  waiting for transfers between devices: 85.3 us -> 0 us
  Pallas kernels: 0 us -> 31.9 us
  matrix products: 6.68 us -> 0 us
  starting transfers between devices: 3.16 us -> 0 us
  local copies, waits for them, and re-layouts: 1.11 us -> 3.84 us
    ppermute x9 -> x0, waiting for transfers between devices: 85.3 us -> none  [shifted(): return lax.ppermute(value, axis, pairs)]
    pallas_call x0 -> x1, Pallas kernels: none -> 31.9 us  [local(): pl.pallas_call(kernel, out_shape=(block, block), in_specs=[pl.BlockSpec(m...]
    dot_general x15 -> x0, matrix products: 6.68 us -> none  [the longest x5 2.76 us: local(): lax.dot_general(image_emb, text_block, (((1,), (1,)), ((), ())), preferre...]
    ppermute x9 -> x0, starting transfers between devices: 3.16 us -> none  [shifted(): return lax.ppermute(value, axis, pairs)]
    unnamed x5 -> x6, local copies, waits for them, and re-layouts: 1.11 us -> 3.84 us
  transfers between devices with their start and end apart: 9 -> 0, of which waited for: 8 -> 0; matrix products, arithmetic and copies ran while one was open for 5% -> 0% of each run, Pallas kernels for 0% -> 0%
where the time goes in v1:
time: 37.9 us; the launch traced here: 37.6 us
  Pallas kernels  31.9 us (84%)
  local copies, waits for them, and re-layouts  3.84 us (10%)
  between operations  1.94 us (5%)
    pallas_call x1, Pallas kernels, local(): pl.pallas_call(kernel, out_shape=(block, block), in_specs=[pl.BlockSpec(m...  31.9 us
    unnamed x6, local copies, waits for them, and re-layouts  3.84 us

profile of v1, /device:TPU:0, one launch (start us, length us, event | category | flops | bytes accessed | tf_op | source)
XLA Modules:
  0.0 37.6 jit_solution(4294100468396822094)
XLA Ops:
  1.9 0.0 copy-start
  1.9 1.0 %copy-done = bf16[192,1152]{1,0:T(8,128)(2,1)S(1)} copy-done((bf16[192,1152]{1,0:T(8,128)(2,1)S(1)}, bf16[192,1152]{1,0:T(8,128)(2,1)}, u32[]{:S(2)}) %copy-start) | copy-done | bytes 442392
  2.9 0.0 copy-start.1
  2.9 1.0 %copy-done.1 = bf16[192,1152]{1,0:T(8,128)(2,1)S(1)} copy-done((bf16[192,1152]{1,0:T(8,128)(2,1)S(1)}, bf16[192,1152]{1,0:T(8,128)(2,1)}, u32[]{:S(2)}) %copy-start.1) | copy-done | bytes 442392
  3.9 31.9 %shard_map.59 = (f32[192,1152]{1,0:T(8,128)S(1)}, f32[192,1152]{1,0:T(8,128)S(1)}) custom-call(f32[1]{0:T(128)S(6)} %copy.8.log_scale_ref, f32[1]{0:T(128)S(6)} %copy.9.bias_ref, bf16[192,1152]{1,0:T(8,128)(2,1)S(1)} %copy-done, bf16[192,1152]{1,0:T(8,128)(2,1)S(1)} %copy-done.1), custom_call_target="tpu_custom_call" | custom-call | flops 1698693120 | bytes 2654208 | tf_op jit(solution)/shard_map/pallas_call | solution.py:155
  35.8 0.9 %copy.10 = f32[192,1152]{1,0:T(8,128)} copy(f32[192,1152]{1,0:T(8,128)S(1)} %get-tuple-element.4) | data formatting | bytes 1769472
  36.7 0.9 %copy.11 = f32[192,1152]{1,0:T(8,128)} copy(f32[192,1152]{1,0:T(8,128)S(1)} %get-tuple-element.5) | data formatting | bytes 1769472
Async XLA Ops:
  1.9 1.0 %copy-start = (bf16[192,1152]{1,0:T(8,128)(2,1)S(1)}, bf16[192,1152]{1,0:T(8,128)(2,1)}, u32[]{:S(2)}) copy-start(bf16[192,1152]{1,0:T(8,128)(2,1)} %image_ref.1) | copy-start | bytes 1327108
  2.9 1.0 %copy-start.1 = (bf16[192,1152]{1,0:T(8,128)(2,1)S(1)}, bf16[192,1152]{1,0:T(8,128)(2,1)}, u32[]{:S(2)}) copy-start(bf16[192,1152]{1,0:T(8,128)(2,1)} %text_ref.1) | copy-start | bytes 1327108

commit v2 on v1

--- a/solution.py
+++ b/solution.py
@@ -73,7 +73,6 @@
         far_first[i].start()
         near_own[i].start()
     for i in range(CHUNKS):
-        far_second[i].start()
         core_own[i].start()
 
     scale = jnp.exp(jnp.full((1, rows), log_scale_ref[0], jnp.float32))
@@ -102,6 +101,7 @@
     for i in range(CHUNKS):
         far_first[i].wait_recv()
         near_far[i].start()
+        far_second[i].start()
 
         @pl.when(side == core)
         def _():
@@ -171,7 +171,7 @@
             pltpu.SemaphoreType.DMA((8, CHUNKS)),
         ],
         compiler_params=pltpu.CompilerParams(
-            collective_id=0, has_side_effects=True, vmem_limit_bytes=32 * 1024 * 1024
+            collective_id=0, has_side_effects=True, vmem_limit_bytes=60 * 1024 * 1024
         ),
         cost_estimate=pl.CostEstimate(
             flops=20 * 2 * rows * rows * width, bytes_accessed=12 * rows * width, transcendentals=9 * rows * rows

time: 37.9 us -> 39.4 us (1.040)
  the two profiles are of different devices: /device:TPU:0 before, /device:TPU:3 now
where the time goes in v2:
time: 39.4 us; the launch traced here: 39.2 us
  Pallas kernels  34.2 us (87%)
  local copies, waits for them, and re-layouts  3.13 us (8%)
  between operations  1.94 us (5%)
    pallas_call x1, Pallas kernels, local(): pl.pallas_call(kernel, out_shape=(block, block), in_specs=[pl.BlockSpec(m...  34.2 us
    unnamed x4, local copies, waits for them, and re-layouts  3.13 us

profile of v2, /device:TPU:3, one launch (start us, length us, event | category | flops | bytes accessed | tf_op | source)
XLA Modules:
  0.0 39.2 jit_solution(10684581612074887592)
XLA Ops:
  1.9 34.2 %shard_map.59 = (f32[192,1152]{1,0:T(8,128)}, f32[192,1152]{1,0:T(8,128)}) custom-call(f32[1]{0:T(128)S(6)} %copy.8.log_scale_ref, f32[1]{0:T(128)S(6)} %copy.9.bias_ref, bf16[192,1152]{1,0:T(8,128)(2,1)} %image_ref.1, bf16[192,1152]{1,0:T(8,128)(2,1)} %text_ref.1), custom_call_target="tpu_custom_call" | custom-call | flops 1698693120 | bytes 2654208 | tf_op jit(solution)/shard_map/pallas_call | solution.py:155
  36.1 0.0 copy-start
  36.1 2.2 %copy.10 = f32[192,1152]{1,0:T(8,128)} copy(f32[192,1152]{1,0:T(8,128)} %get-tuple-element.4) | data formatting | bytes 1769472
  38.3 0.0 copy-done
  38.3 0.9 %copy.11 = f32[192,1152]{1,0:T(8,128)} copy(f32[192,1152]{1,0:T(8,128)S(1)} %copy-done) | data formatting | bytes 1769472
Async XLA Ops:
  36.1 2.2 %copy-start = (f32[192,1152]{1,0:T(8,128)S(1)}, f32[192,1152]{1,0:T(8,128)}, u32[]{:S(2)}) copy-start(f32[192,1152]{1,0:T(8,128)} %get-tuple-element.5) | copy-start | bytes 2654212

commit v3 on v1

v3 whole, which is shorter than its diff:
```python
import jax
import jax.numpy as jnp
from jax import lax
from jax.experimental import pallas as pl
from jax.experimental.pallas import tpu as pltpu
from jax.sharding import PartitionSpec as P

SHIFTS = 4
CHUNKS = 3

FAR_FIRST = 0
NEAR_OWN = 1
CORE_NEAR_OWN = 2
FAR_SECOND = 3
NEAR_FAR = 4
CORE_NEAR_FAR = 5
CORE_OWN = 6
CORE_FAR = 7


def kernel(
    log_scale_ref, bias_ref, image_ref, text_ref, total,
    own, turned, held, twin_held, load_sem, send_sem, recv_sem,
):
    dp_count, mp_count = lax.axis_size("dp"), lax.axis_size("mp")
    count = dp_count * mp_count
    me = lax.axis_index("dp") * mp_count + lax.axis_index("mp")
    core = lax.rem(me, 2)
    side = lax.rem(me // 2, 2)
    rows, width = image_ref.shape
    part = rows // CHUNKS

    def place(index):
        return (index // mp_count, lax.rem(index, mp_count))

    after = place(lax.rem(me + SHIFTS, count))
    before = place(lax.rem(me + count - SHIFTS, count))
    near = place(me + 2 - 4 * side)
    twin = place(me + 1 - 2 * core)

    loads = [
        pltpu.make_async_copy(image_ref, own.at[0], load_sem.at[0]),
        pltpu.make_async_copy(text_ref, own.at[1], load_sem.at[1]),
    ]
    for load in loads:
        load.start()

    barrier = pltpu.get_barrier_semaphore()
    for other in (after, before, near, twin):
        pl.semaphore_signal(barrier, inc=1, device_id=other, device_id_type=pl.DeviceIdType.MESH)
    pl.semaphore_wait(barrier, 4)
    for load in loads:
        load.wait()

    def remote(source, target, slot, chunk, device):
        return pltpu.make_async_remote_copy(
            src_ref=source,
            dst_ref=target,
            send_sem=send_sem.at[slot, chunk],
            recv_sem=recv_sem.at[slot, chunk],
            device_id=device,
            device_id_type=pl.DeviceIdType.MESH,
        )

    def span(chunk):
        return pl.ds(chunk * part, part)

    def far(kind, slot, chunk):
        device = tuple(jnp.where(kind == 0, b, a) for a, b in zip(after, before))
        return remote(own.at[kind, span(chunk)], held.at[chunk, slot], slot, chunk, device)

    first, second = side, 1 - side
    chunks = range(CHUNKS)
    far_first = [far(first, FAR_FIRST, i) for i in chunks]
    far_second = [far(second, FAR_SECOND, i) for i in chunks]
    near_own = [remote(own.at[1 - side, span(i)], held.at[i, NEAR_OWN], NEAR_OWN, i, near) for i in chunks]
    near_far = [remote(held.at[i, FAR_FIRST], held.at[i, NEAR_FAR], NEAR_FAR, i, near) for i in chunks]
    core_near_own = [remote(held.at[i, NEAR_OWN], held.at[i, CORE_NEAR_OWN], CORE_NEAR_OWN, i, twin) for i in chunks]
    core_near_far = [remote(held.at[i, NEAR_FAR], held.at[i, CORE_NEAR_FAR], CORE_NEAR_FAR, i, twin) for i in chunks]
    core_own = [remote(own.at[1 - core, span(i)], twin_held.at[0, span(i)], CORE_OWN, i, twin) for i in chunks]
    far_slot = jnp.where(side == core, FAR_FIRST, FAR_SECOND)
    core_far = [remote(held.at[i, far_slot], twin_held.at[1, span(i)], CORE_FAR, i, twin) for i in chunks]

    for i in chunks:
        far_first[i].start()
        near_own[i].start()
    for i in chunks:
        core_own[i].start()
    far_second[0].start()

    scale = jnp.exp(jnp.full((1, rows), log_scale_ref[0], jnp.float32))
    offset = bias_ref[0]
    for kind in range(2):
        turned[kind] = own[kind].T

    def weights_of(block, kind):
        inner = jnp.dot(block, turned[1 - kind], preferred_element_type=jnp.float32)
        return jax.nn.sigmoid(scale * inner + offset)

    def add(block, kind):
        weights = (scale * weights_of(block, kind)).astype(jnp.bfloat16)
        total[1 - kind] += lax.dot_general(
            weights, block, (((0,), (0,)), ((), ())), preferred_element_type=jnp.float32
        )

    row_ids = lax.broadcasted_iota(jnp.int32, (rows, rows), 0)
    col_ids = lax.broadcasted_iota(jnp.int32, (rows, rows), 1)
    target = jnp.where(row_ids == col_ids, 1.0, 0.0).astype(jnp.float32)
    own_weights = (scale * (weights_of(own[0], 0) - target)).astype(jnp.bfloat16)
    total[0] = jnp.dot(own_weights, own[1], preferred_element_type=jnp.float32)
    total[1] = lax.dot_general(own_weights, own[0], (((0,), (0,)), ((), ())), preferred_element_type=jnp.float32)

    for copy in core_own:
        copy.wait_recv()
    add(twin_held[0], core)

    for i in chunks:
        far_first[i].wait_recv()
        near_far[i].start()

        @pl.when(side == core)
        def _():
            core_far[i].start()

        if i + 1 < CHUNKS:
            far_second[i + 1].start()
        near_own[i].wait_recv()
        core_near_own[i].start()

    for i in chunks:
        core_near_own[i].wait_recv()
        add(held[i, 0:3].reshape(3 * part, width), side)

    for i in chunks:
        near_far[i].wait_recv()
        core_near_far[i].start()
        far_second[i].wait_recv()

        @pl.when(side != core)
        def _():
            core_far[i].start()

        if i + 1 == CHUNKS:
            for copy in core_far[:-1]:
                copy.wait_recv()
            add(twin_held[1, : rows - part], 1 - core)
        core_near_far[i].wait_recv()
        add(held[i, 3:6].reshape(3 * part, width), 1 - side)

    core_far[-1].wait_recv()
    add(twin_held[1, rows - part :], 1 - core)

    for copies in (far_first, far_second, near_own, near_far, core_own, core_far, core_near_own, core_near_far):
        for copy in copies:
            copy.wait_send()


def write_out(total, image_out, text_out, store_sem):
    stores = [
        pltpu.make_async_copy(total.at[0], image_out, store_sem.at[0]),
        pltpu.make_async_copy(total.at[1], text_out, store_sem.at[1]),
    ]
    for store in stores:
        store.start()
    for store in stores:
        store.wait()


def local(image_emb, text_emb, log_scale, bias):
    rows, width = image_emb.shape
    block = jax.ShapeDtypeStruct((rows, width), jnp.float32)
    part = rows // CHUNKS
    in_hbm = [pltpu.with_memory_space_constraint(value, pltpu.HBM) for value in (image_emb, text_emb)]
    total = pl.pallas_call(
        kernel,
        out_shape=pltpu.VMEM((2, rows, width), jnp.float32),
        in_specs=[pl.BlockSpec(memory_space=pltpu.SMEM)] * 2 + [pl.BlockSpec(memory_space=pl.ANY)] * 2,
        out_specs=pl.BlockSpec(memory_space=pltpu.VMEM),
        scratch_shapes=[
            pltpu.VMEM((2, rows, width), jnp.bfloat16),
            pltpu.VMEM((2, width, rows), jnp.bfloat16),
            pltpu.VMEM((CHUNKS, 6, part, width), jnp.bfloat16),
            pltpu.VMEM((2, rows, width), jnp.bfloat16),
            pltpu.SemaphoreType.DMA((2,)),
            pltpu.SemaphoreType.DMA((8, CHUNKS)),
            pltpu.SemaphoreType.DMA((8, CHUNKS)),
        ],
        compiler_params=pltpu.CompilerParams(
            collective_id=0, has_side_effects=True, vmem_limit_bytes=32 * 1024 * 1024
        ),
        cost_estimate=pl.CostEstimate(
            flops=20 * 2 * rows * rows * width, bytes_accessed=12 * rows * width, transcendentals=9 * rows * rows
        ),
    )(log_scale, bias, *in_hbm)
    return pl.pallas_call(
        write_out,
        out_shape=(block, block),
        in_specs=[pl.BlockSpec(memory_space=pltpu.VMEM)],
        out_specs=(pl.BlockSpec(memory_space=pl.ANY), pl.BlockSpec(memory_space=pl.ANY)),
        scratch_shapes=[pltpu.SemaphoreType.DMA((2,))],
        cost_estimate=pl.CostEstimate(flops=0, bytes_accessed=16 * rows * width, transcendentals=0),
    )(total)


def solution(mesh):
    count = 1
    for axis in ("dp", "mp"):
        count *= mesh.shape[axis]
    assert mesh.shape["mp"] % 4 == 0 and count > 2 * SHIFTS
    return jax.shard_map(
        local,
        mesh=mesh,
        in_specs=(P(("dp", "mp"), None), P(("dp", "mp"), None), P(), P()),
        out_specs=(P(("dp", "mp"), None), P(("dp", "mp"), None)),
        check_vma=False,
    )
```

time: 37.9 us -> 38.9 us (1.026)
  Pallas kernels: 31.9 us -> 35.6 us
  local copies, waits for them, and re-layouts: 3.84 us -> 1.22 us
    pallas_call x1 -> x2, Pallas kernels: 31.9 us -> 35.6 us  [the longest x1 32.9 us: local(): pl.pallas_call(kernel, out_shape=pltpu.VMEM((2, rows, width), jnp.float32...]
    unnamed x6 -> x2, local copies, waits for them, and re-layouts: 3.84 us -> 1.22 us
where the time goes in v3:
time: 38.9 us; the launch traced here: 38.8 us
  Pallas kernels  35.6 us (92%)
  between operations  1.94 us (5%)
  local copies, waits for them, and re-layouts  1.22 us (3%)
    pallas_call x1, Pallas kernels, local(): pl.pallas_call(kernel, out_shape=pltpu.VMEM((2, rows, width), jnp.float32...  32.9 us
    pallas_call x1, Pallas kernels, local(): pl.pallas_call(write_out, out_shape=(block, block), in_specs=[pl.BlockSpe...  2.69 us
    unnamed x2, local copies, waits for them, and re-layouts  1.22 us

profile of v3, /device:TPU:0, one launch (start us, length us, event | category | flops | bytes accessed | tf_op | source)
XLA Modules:
  0.0 38.8 jit_solution(13727535109151160588)
XLA Ops:
  1.9 32.9 %shard_map.59.total = f32[2,192,1152]{2,1,0:T(8,128)S(1)} custom-call(f32[1]{0:T(128)S(6)} %copy.6.log_scale_ref, f32[1]{0:T(128)S(6)} %copy.7.bias_ref, bf16[192,1152]{1,0:T(8,128)(2,1)} %image_ref.1, bf16[192,1152]{1,0:T(8,128)(2,1)} %text_ref.1), custom_call_target="tpu_custom_call" | custom-call | flops 1698693120 | bytes 2654208 | tf_op jit(solution)/shard_map/pallas_call | solution.py:174
  34.8 0.0 copy-start
  34.9 1.2 %copy-done = f32[2,192,1152]{2,1,0:T(8,128)} copy-done((f32[2,192,1152]{2,1,0:T(8,128)}, f32[2,192,1152]{2,1,0:T(8,128)S(1)}, u32[]{:S(2)}) %copy-start) | copy-done | bytes 1769496
  36.1 2.7 %shard_map.60 = (f32[192,1152]{1,0:T(8,128)}, f32[192,1152]{1,0:T(8,128)}) custom-call(f32[2,192,1152]{2,1,0:T(8,128)} %copy-done), custom_call_target="tpu_custom_call" | custom-call | bytes 3538944 | tf_op jit(solution)/shard_map/pallas_call | solution.py:195
Async XLA Ops:
  34.8 1.2 %copy-start = (f32[2,192,1152]{2,1,0:T(8,128)}, f32[2,192,1152]{2,1,0:T(8,128)S(1)}, u32[]{:S(2)}) copy-start(f32[2,192,1152]{2,1,0:T(8,128)S(1)} %shard_map.59.total) | copy-start | bytes 5308420

commit v4 on v3

--- a/solution.py
+++ b/solution.py
@@ -6,7 +6,10 @@
 from jax.sharding import PartitionSpec as P
 
 SHIFTS = 4
-CHUNKS = 3
+SIZES = (32, 64, 64, 32)
+STARTS = (0, 32, 96, 160)
+CHUNKS = len(SIZES)
+DEPTH = 2
 
 FAR_FIRST = 0
 NEAR_OWN = 1
@@ -20,7 +23,7 @@
 
 def kernel(
     log_scale_ref, bias_ref, image_ref, text_ref, total,
-    own, turned, held, twin_held, load_sem, send_sem, recv_sem,
+    own, turned, *scratch,
 ):
     dp_count, mp_count = lax.axis_size("dp"), lax.axis_size("mp")
     count = dp_count * mp_count
@@ -28,7 +31,8 @@
     core = lax.rem(me, 2)
     side = lax.rem(me // 2, 2)
     rows, width = image_ref.shape
-    part = rows // CHUNKS
+    held = scratch[:CHUNKS]
+    twin_held, load_sem, send_sem, recv_sem = scratch[CHUNKS:]
 
     def place(index):
         return (index // mp_count, lax.rem(index, mp_count))
@@ -63,30 +67,31 @@
         )
 
     def span(chunk):
-        return pl.ds(chunk * part, part)
+        return pl.ds(STARTS[chunk], SIZES[chunk])
 
     def far(kind, slot, chunk):
         device = tuple(jnp.where(kind == 0, b, a) for a, b in zip(after, before))
-        return remote(own.at[kind, span(chunk)], held.at[chunk, slot], slot, chunk, device)
+        return remote(own.at[kind, span(chunk)], held[chunk].at[slot], slot, chunk, device)
 
     first, second = side, 1 - side
     chunks = range(CHUNKS)
-    far_first = [far(first, FAR_FIRST, i) for i in chunks]
-    far_second = [far(second, FAR_SECOND, i) for i in chunks]
-    near_own = [remote(own.at[1 - side, span(i)], held.at[i, NEAR_OWN], NEAR_OWN, i, near) for i in chunks]
-    near_far = [remote(held.at[i, FAR_FIRST], held.at[i, NEAR_FAR], NEAR_FAR, i, near) for i in chunks]
-    core_near_own = [remote(held.at[i, NEAR_OWN], held.at[i, CORE_NEAR_OWN], CORE_NEAR_OWN, i, twin) for i in chunks]
-    core_near_far = [remote(held.at[i, NEAR_FAR], held.at[i, CORE_NEAR_FAR], CORE_NEAR_FAR, i, twin) for i in chunks]
+
+    def passed(source, slot, device):
+        return [remote(held[i].at[source], held[i].at[slot], slot, i, device) for i in chunks]
+
+    far_stream = [far(first, FAR_FIRST, i) for i in chunks] + [far(second, FAR_SECOND, i) for i in chunks]
+    near_stream = [remote(own.at[1 - side, span(i)], held[i].at[NEAR_OWN], NEAR_OWN, i, near) for i in chunks]
+    near_stream += passed(FAR_FIRST, NEAR_FAR, near)
+    twin_stream = passed(NEAR_OWN, CORE_NEAR_OWN, twin) + passed(NEAR_FAR, CORE_NEAR_FAR, twin)
     core_own = [remote(own.at[1 - core, span(i)], twin_held.at[0, span(i)], CORE_OWN, i, twin) for i in chunks]
     far_slot = jnp.where(side == core, FAR_FIRST, FAR_SECOND)
-    core_far = [remote(held.at[i, far_slot], twin_held.at[1, span(i)], CORE_FAR, i, twin) for i in chunks]
-
-    for i in chunks:
-        far_first[i].start()
-        near_own[i].start()
-    for i in chunks:
-        core_own[i].start()
-    far_second[0].start()
+    core_far = [remote(held[i].at[far_slot], twin_held.at[1, span(i)], CORE_FAR, i, twin) for i in chunks]
+
+    for i in range(DEPTH):
+        far_stream[i].start()
+        near_stream[i].start()
+    for copy in core_own:
+        copy.start()
 
     scale = jnp.exp(jnp.full((1, rows), log_scale_ref[0], jnp.float32))
     offset = bias_ref[0]
@@ -102,6 +107,12 @@
         total[1 - kind] += lax.dot_general(
             weights, block, (((0,), (0,)), ((), ())), preferred_element_type=jnp.float32
         )
+
+    def add_batch(step):
+        twin_stream[step].wait_recv()
+        chunk, late = step % CHUNKS, step // CHUNKS
+        block = held[chunk][3 * late : 3 * late + 3].reshape(3 * SIZES[chunk], width)
+        add(block, second if late else first)
 
     row_ids = lax.broadcasted_iota(jnp.int32, (rows, rows), 0)
     col_ids = lax.broadcasted_iota(jnp.int32, (rows, rows), 1)
@@ -110,47 +121,38 @@
     total[0] = jnp.dot(own_weights, own[1], preferred_element_type=jnp.float32)
     total[1] = lax.dot_general(own_weights, own[0], (((0,), (0,)), ((), ())), preferred_element_type=jnp.float32)
 
-    for copy in core_own:
+    steps = 2 * CHUNKS
+    for step in range(steps):
+        far_stream[step].wait_send()
+        if step + DEPTH < steps:
+            far_stream[step + DEPTH].start()
+        near_stream[step].wait_send()
+        if step + DEPTH < steps:
+            near_stream[step + DEPTH].start()
+        near_stream[step].wait_recv()
+        twin_stream[step].start()
+        far_stream[step].wait_recv()
+
+        @pl.when((side == core) if step < CHUNKS else (side != core))
+        def _():
+            core_far[step % CHUNKS].start()
+
+        if step == 0:
+            for copy in core_own:
+                copy.wait_recv()
+            add(twin_held[0], core)
+        else:
+            add_batch(step - 1)
+
+    early = STARTS[-1]
+    for copy in core_far[:-1]:
         copy.wait_recv()
-    add(twin_held[0], core)
-
-    for i in chunks:
-        far_first[i].wait_recv()
-        near_far[i].start()
-
-        @pl.when(side == core)
-        def _():
-            core_far[i].start()
-
-        if i + 1 < CHUNKS:
-            far_second[i + 1].start()
-        near_own[i].wait_recv()
-        core_near_own[i].start()
-
-    for i in chunks:
-        core_near_own[i].wait_recv()
-        add(held[i, 0:3].reshape(3 * part, width), side)
-
-    for i in chunks:
-        near_far[i].wait_recv()
-        core_near_far[i].start()
-        far_second[i].wait_recv()
-
-        @pl.when(side != core)
-        def _():
-            core_far[i].start()
-
-        if i + 1 == CHUNKS:
-            for copy in core_far[:-1]:
-                copy.wait_recv()
-            add(twin_held[1, : rows - part], 1 - core)
-        core_near_far[i].wait_recv()
-        add(held[i, 3:6].reshape(3 * part, width), 1 - side)
-
+    add(twin_held[1, :early], 1 - core)
+    add_batch(steps - 1)
     core_far[-1].wait_recv()
-    add(twin_held[1, rows - part :], 1 - core)
-
-    for copies in (far_first, far_second, near_own, near_far, core_own, core_far, core_near_own, core_near_far):
+    add(twin_held[1, early:], 1 - core)
+
+    for copies in (twin_stream, core_own, core_far):
         for copy in copies:
             copy.wait_send()
 
@@ -169,7 +171,7 @@
 def local(image_emb, text_emb, log_scale, bias):
     rows, width = image_emb.shape
     block = jax.ShapeDtypeStruct((rows, width), jnp.float32)
-    part = rows // CHUNKS
+    assert rows == sum(SIZES)
     in_hbm = [pltpu.with_memory_space_constraint(value, pltpu.HBM) for value in (image_emb, text_emb)]
     total = pl.pallas_call(
         kernel,
@@ -179,7 +181,7 @@
         scratch_shapes=[
             pltpu.VMEM((2, rows, width), jnp.bfloat16),
             pltpu.VMEM((2, width, rows), jnp.bfloat16),
-            pltpu.VMEM((CHUNKS, 6, part, width), jnp.bfloat16),
+            *[pltpu.VMEM((6, size, width), jnp.bfloat16) for size in SIZES],
             pltpu.VMEM((2, rows, width), jnp.bfloat16),
             pltpu.SemaphoreType.DMA((2,)),
             pltpu.SemaphoreType.DMA((8, CHUNKS)),
@@ -195,9 +197,10 @@
     return pl.pallas_call(
         write_out,
         out_shape=(block, block),
-        in_specs=[pl.BlockSpec(memory_space=pltpu.VMEM)],
+        in_specs=[pl.BlockSpec(memory_space=pl.ANY)],
         out_specs=(pl.BlockSpec(memory_space=pl.ANY), pl.BlockSpec(memory_space=pl.ANY)),
         scratch_shapes=[pltpu.SemaphoreType.DMA((2,))],
+        compiler_params=pltpu.CompilerParams(vmem_limit_bytes=1024 * 1024),
         cost_estimate=pl.CostEstimate(flops=0, bytes_accessed=16 * rows * width, transcendentals=0),
     )(total)
 

time: 38.9 us -> 41.8 us (1.075)
  Pallas kernels: 35.6 us -> 39.6 us
  local copies, waits for them, and re-layouts: 1.22 us -> 0 us
    pallas_call x1, Pallas kernels: 32.9 us -> 38.4 us  [local(): pl.pallas_call(kernel, out_shape=pltpu.VMEM((2, rows, width), jnp.float32...]
    pallas_call x1, Pallas kernels: 2.69 us -> 1.22 us  [local(): pl.pallas_call(write_out, out_shape=(block, block), in_specs=[pl.BlockSpe...]
    unnamed x2 -> x0, local copies, waits for them, and re-layouts: 1.22 us -> none
where the time goes in v4:
time: 41.8 us; the launch traced here: 41.5 us
  Pallas kernels  39.6 us (95%)
  between operations  1.93 us (5%)
    pallas_call x1, Pallas kernels, local(): pl.pallas_call(kernel, out_shape=pltpu.VMEM((2, rows, width), jnp.float32...  38.4 us
    pallas_call x1, Pallas kernels, local(): pl.pallas_call(write_out, out_shape=(block, block), in_specs=[pl.BlockSpe...  1.22 us

profile of v4, /device:TPU:0, one launch (start us, length us, event | category | flops | bytes accessed | tf_op | source)
XLA Modules:
  0.0 41.5 jit_solution(8435860862026339674)
XLA Ops:
  1.9 38.4 %shard_map.59.total = f32[2,192,1152]{2,1,0:T(8,128)S(1)} custom-call(f32[1]{0:T(128)S(6)} %copy.6.log_scale_ref, f32[1]{0:T(128)S(6)} %copy.7.bias_ref, bf16[192,1152]{1,0:T(8,128)(2,1)} %image_ref.1, bf16[192,1152]{1,0:T(8,128)(2,1)} %text_ref.1), custom_call_target="tpu_custom_call" | custom-call | flops 1698693120 | bytes 2654208 | tf_op jit(solution)/shard_map/pallas_call | solution.py:176
  40.3 1.2 %shard_map.60 = (f32[192,1152]{1,0:T(8,128)}, f32[192,1152]{1,0:T(8,128)}) custom-call(f32[2,192,1152]{2,1,0:T(8,128)S(1)} %shard_map.59.total), custom_call_target="tpu_custom_call" | custom-call | bytes 3538944 | tf_op jit(solution)/shard_map/pallas_call | solution.py:197

commit v5 on v4

--- a/solution.py
+++ b/solution.py
@@ -9,7 +9,7 @@
 SIZES = (32, 64, 64, 32)
 STARTS = (0, 32, 96, 160)
 CHUNKS = len(SIZES)
-DEPTH = 2
+FAR_DEPTH, NEAR_DEPTH = 4, 3
 
 FAR_FIRST = 0
 NEAR_OWN = 1
@@ -87,9 +87,10 @@
     far_slot = jnp.where(side == core, FAR_FIRST, FAR_SECOND)
     core_far = [remote(held[i].at[far_slot], twin_held.at[1, span(i)], CORE_FAR, i, twin) for i in chunks]
 
-    for i in range(DEPTH):
+    for i in range(FAR_DEPTH):
         far_stream[i].start()
-        near_stream[i].start()
+        if i < NEAR_DEPTH:
+            near_stream[i].start()
     for copy in core_own:
         copy.start()
 
@@ -123,14 +124,14 @@
 
     steps = 2 * CHUNKS
     for step in range(steps):
-        far_stream[step].wait_send()
-        if step + DEPTH < steps:
-            far_stream[step + DEPTH].start()
         near_stream[step].wait_send()
-        if step + DEPTH < steps:
-            near_stream[step + DEPTH].start()
+        if step + NEAR_DEPTH < steps:
+            near_stream[step + NEAR_DEPTH].start()
         near_stream[step].wait_recv()
         twin_stream[step].start()
+        far_stream[step].wait_send()
+        if step + FAR_DEPTH < steps:
+            far_stream[step + FAR_DEPTH].start()
         far_stream[step].wait_recv()
 
         @pl.when((side == core) if step < CHUNKS else (side != core))

time: 41.8 us -> 37.9 us (0.907)
  Pallas kernels: 39.6 us -> 35.6 us
    pallas_call x1, Pallas kernels: 38.4 us -> 34.4 us  [local(): pl.pallas_call(kernel, out_shape=pltpu.VMEM((2, rows, width), jnp.float32...]
where the time goes in v5:
time: 37.9 us; the launch traced here: 37.5 us
  Pallas kernels  35.6 us (94%)
  between operations  1.93 us (5%)
    pallas_call x1, Pallas kernels, local(): pl.pallas_call(kernel, out_shape=pltpu.VMEM((2, rows, width), jnp.float32...  34.4 us
    pallas_call x1, Pallas kernels, local(): pl.pallas_call(write_out, out_shape=(block, block), in_specs=[pl.BlockSpe...  1.22 us

profile of v5, /device:TPU:0, one launch (start us, length us, event | category | flops | bytes accessed | tf_op | source)
XLA Modules:
  0.0 37.5 jit_solution(9896852109916659948)
XLA Ops:
  1.9 34.4 %shard_map.59.total = f32[2,192,1152]{2,1,0:T(8,128)S(1)} custom-call(f32[1]{0:T(128)S(6)} %copy.6.log_scale_ref, f32[1]{0:T(128)S(6)} %copy.7.bias_ref, bf16[192,1152]{1,0:T(8,128)(2,1)} %image_ref.1, bf16[192,1152]{1,0:T(8,128)(2,1)} %text_ref.1), custom_call_target="tpu_custom_call" | custom-call | flops 1698693120 | bytes 2654208 | tf_op jit(solution)/shard_map/pallas_call | solution.py:177
  36.3 1.2 %shard_map.60 = (f32[192,1152]{1,0:T(8,128)}, f32[192,1152]{1,0:T(8,128)}) custom-call(f32[2,192,1152]{2,1,0:T(8,128)S(1)} %shard_map.59.total), custom_call_target="tpu_custom_call" | custom-call | bytes 3538944 | tf_op jit(solution)/shard_map/pallas_call | solution.py:198

commit v6 on v4

--- a/solution.py
+++ b/solution.py
@@ -9,7 +9,6 @@
 SIZES = (32, 64, 64, 32)
 STARTS = (0, 32, 96, 160)
 CHUNKS = len(SIZES)
-DEPTH = 2
 
 FAR_FIRST = 0
 NEAR_OWN = 1
@@ -87,11 +86,21 @@
     far_slot = jnp.where(side == core, FAR_FIRST, FAR_SECOND)
     core_far = [remote(held[i].at[far_slot], twin_held.at[1, span(i)], CORE_FAR, i, twin) for i in chunks]
 
-    for i in range(DEPTH):
-        far_stream[i].start()
-        near_stream[i].start()
-    for copy in core_own:
-        copy.start()
+    far_first, far_second = far_stream[:CHUNKS], far_stream[CHUNKS:]
+    near_own, near_far = near_stream[:CHUNKS], near_stream[CHUNKS:]
+
+    def start(*groups):
+        for group in groups:
+            for copy in group:
+                copy.start()
+
+    @pl.when(core == 0)
+    def _():
+        start(far_first, core_own, near_own)
+
+    @pl.when(core != 0)
+    def _():
+        start(near_own, core_own, far_first)
 
     scale = jnp.exp(jnp.full((1, rows), log_scale_ref[0], jnp.float32))
     offset = bias_ref[0]
@@ -121,38 +130,61 @@
     total[0] = jnp.dot(own_weights, own[1], preferred_element_type=jnp.float32)
     total[1] = lax.dot_general(own_weights, own[0], (((0,), (0,)), ((), ())), preferred_element_type=jnp.float32)
 
-    steps = 2 * CHUNKS
-    for step in range(steps):
-        far_stream[step].wait_send()
-        if step + DEPTH < steps:
-            far_stream[step + DEPTH].start()
-        near_stream[step].wait_send()
-        if step + DEPTH < steps:
-            near_stream[step + DEPTH].start()
-        near_stream[step].wait_recv()
-        twin_stream[step].start()
-        far_stream[step].wait_recv()
-
-        @pl.when((side == core) if step < CHUNKS else (side != core))
+    for copy in core_own:
+        copy.wait_recv()
+    add(twin_held[0], core)
+
+    def take_far(second_too):
+        for i in chunks:
+            far_first[i].wait_recv()
+            near_far[i].start()
+
+            @pl.when(side == core)
+            def _():
+                core_far[i].start()
+
+        if second_too:
+            start(far_second)
+
+    def take_near():
+        for i in chunks:
+            near_own[i].wait_recv()
+            twin_stream[i].start()
+
+    @pl.when(core == 0)
+    def _():
+        take_far(True)
+        take_near()
+
+    @pl.when(core != 0)
+    def _():
+        take_near()
+        start(far_second)
+        take_far(False)
+
+    for i in chunks:
+        add_batch(i)
+    for i in chunks:
+        near_far[i].wait_recv()
+        twin_stream[CHUNKS + i].start()
+        far_second[i].wait_recv()
+
+        @pl.when(side != core)
         def _():
-            core_far[step % CHUNKS].start()
-
-        if step == 0:
-            for copy in core_own:
-                copy.wait_recv()
-            add(twin_held[0], core)
-        else:
-            add_batch(step - 1)
+            core_far[i].start()
+
+        if i > 0:
+            add_batch(CHUNKS + i - 1)
 
     early = STARTS[-1]
     for copy in core_far[:-1]:
         copy.wait_recv()
     add(twin_held[1, :early], 1 - core)
-    add_batch(steps - 1)
+    add_batch(2 * CHUNKS - 1)
     core_far[-1].wait_recv()
     add(twin_held[1, early:], 1 - core)
 
-    for copies in (twin_stream, core_own, core_far):
+    for copies in (far_stream, near_stream, twin_stream, core_own, core_far):
         for copy in copies:
             copy.wait_send()
 

time: 41.8 us -> 39 us (0.933)
  the two profiles are of different devices: /device:TPU:0 before, /device:TPU:3 now
where the time goes in v6:
time: 39 us; the launch traced here: 38.9 us
  Pallas kernels  36.9 us (95%)
  between operations  1.93 us (5%)
    pallas_call x1, Pallas kernels, local(): pl.pallas_call(kernel, out_shape=pltpu.VMEM((2, rows, width), jnp.float32...  35.7 us
    pallas_call x1, Pallas kernels, local(): pl.pallas_call(write_out, out_shape=(block, block), in_specs=[pl.BlockSpe...  1.22 us

profile of v6, /device:TPU:3, one launch (start us, length us, event | category | flops | bytes accessed | tf_op | source)
XLA Modules:
  0.0 38.9 jit_solution(7150913576752128919)
XLA Ops:
  1.9 35.7 %shard_map.59.total = f32[2,192,1152]{2,1,0:T(8,128)S(1)} custom-call(f32[1]{0:T(128)S(6)} %copy.6.log_scale_ref, f32[1]{0:T(128)S(6)} %copy.7.bias_ref, bf16[192,1152]{1,0:T(8,128)(2,1)} %image_ref.1, bf16[192,1152]{1,0:T(8,128)(2,1)} %text_ref.1), custom_call_target="tpu_custom_call" | custom-call | flops 1698693120 | bytes 2654208 | tf_op jit(solution)/shard_map/pallas_call | solution.py:208
  37.6 1.2 %shard_map.60 = (f32[192,1152]{1,0:T(8,128)}, f32[192,1152]{1,0:T(8,128)}) custom-call(f32[2,192,1152]{2,1,0:T(8,128)S(1)} %shard_map.59.total), custom_call_target="tpu_custom_call" | custom-call | bytes 3538944 | tf_op jit(solution)/shard_map/pallas_call | solution.py:229

commit v7 on v6

--- a/solution.py
+++ b/solution.py
@@ -94,13 +94,21 @@
             for copy in group:
                 copy.start()
 
+    second_wraps = jnp.logical_or(
+        jnp.logical_and(second == 0, me < SHIFTS), jnp.logical_and(second == 1, me >= count - SHIFTS)
+    )
+
     @pl.when(core == 0)
     def _():
         start(far_first, core_own, near_own)
 
+        @pl.when(second_wraps)
+        def _():
+            start(far_second)
+
     @pl.when(core != 0)
     def _():
-        start(near_own, core_own, far_first)
+        start(near_own, core_own, far_first, far_second)
 
     scale = jnp.exp(jnp.full((1, rows), log_scale_ref[0], jnp.float32))
     offset = bias_ref[0]
@@ -134,7 +142,7 @@
         copy.wait_recv()
     add(twin_held[0], core)
 
-    def take_far(second_too):
+    def take_far():
         for i in chunks:
             far_first[i].wait_recv()
             near_far[i].start()
@@ -142,9 +150,6 @@
             @pl.when(side == core)
             def _():
                 core_far[i].start()
-
-        if second_too:
-            start(far_second)
 
     def take_near():
         for i in chunks:
@@ -153,14 +158,18 @@
 
     @pl.when(core == 0)
     def _():
-        take_far(True)
+        take_far()
+
+        @pl.when(jnp.logical_not(second_wraps))
+        def _():
+            start(far_second)
+
         take_near()
 
     @pl.when(core != 0)
     def _():
         take_near()
-        start(far_second)
-        take_far(False)
+        take_far()
 
     for i in chunks:
         add_batch(i)

time: 39 us -> 37.1 us (0.951)
  the two profiles are of different devices: /device:TPU:3 before, /device:TPU:0 now
where the time goes in v7:
time: 37.1 us; the launch traced here: 36.7 us
  Pallas kernels  34.8 us (94%)
  between operations  1.93 us (5%)
    pallas_call x1, Pallas kernels, local(): pl.pallas_call(kernel, out_shape=pltpu.VMEM((2, rows, width), jnp.float32...  33.6 us
    pallas_call x1, Pallas kernels, local(): pl.pallas_call(write_out, out_shape=(block, block), in_specs=[pl.BlockSpe...  1.22 us

profile of v7, /device:TPU:0, one launch (start us, length us, event | category | flops | bytes accessed | tf_op | source)
XLA Modules:
  0.0 36.7 jit_solution(11573842736220352644)
XLA Ops:
  1.9 33.6 %shard_map.59.total = f32[2,192,1152]{2,1,0:T(8,128)S(1)} custom-call(f32[1]{0:T(128)S(6)} %copy.6.log_scale_ref, f32[1]{0:T(128)S(6)} %copy.7.bias_ref, bf16[192,1152]{1,0:T(8,128)(2,1)} %image_ref.1, bf16[192,1152]{1,0:T(8,128)(2,1)} %text_ref.1), custom_call_target="tpu_custom_call" | custom-call | flops 1698693120 | bytes 2654208 | tf_op jit(solution)/shard_map/pallas_call | solution.py:217
  35.5 1.2 %shard_map.60 = (f32[192,1152]{1,0:T(8,128)}, f32[192,1152]{1,0:T(8,128)}) custom-call(f32[2,192,1152]{2,1,0:T(8,128)S(1)} %shard_map.59.total), custom_call_target="tpu_custom_call" | custom-call | bytes 3538944 | tf_op jit(solution)/shard_map/pallas_call | solution.py:238

commit v8 on v7

--- a/solution.py
+++ b/solution.py
@@ -102,13 +102,9 @@
     def _():
         start(far_first, core_own, near_own)
 
-        @pl.when(second_wraps)
-        def _():
-            start(far_second)
-
     @pl.when(core != 0)
     def _():
-        start(near_own, core_own, far_first, far_second)
+        start(near_own, core_own, far_first)
 
     scale = jnp.exp(jnp.full((1, rows), log_scale_ref[0], jnp.float32))
     offset = bias_ref[0]
@@ -158,6 +154,12 @@
 
     @pl.when(core == 0)
     def _():
+        @pl.when(second_wraps)
+        def _():
+            for copy in far_first:
+                copy.wait_send()
+            start(far_second)
+
         take_far()
 
         @pl.when(jnp.logical_not(second_wraps))
@@ -169,11 +171,17 @@
     @pl.when(core != 0)
     def _():
         take_near()
+        start(far_second)
         take_far()
 
     for i in chunks:
         add_batch(i)
+    early = STARTS[-1]
     for i in chunks:
+        if i + 1 == CHUNKS:
+            for copy in core_far[:-1]:
+                copy.wait_recv()
+            add(twin_held[1, :early], 1 - core)
         near_far[i].wait_recv()
         twin_stream[CHUNKS + i].start()
         far_second[i].wait_recv()
@@ -185,15 +193,16 @@
         if i > 0:
             add_batch(CHUNKS + i - 1)
 
-    early = STARTS[-1]
-    for copy in core_far[:-1]:
-        copy.wait_recv()
-    add(twin_held[1, :early], 1 - core)
     add_batch(2 * CHUNKS - 1)
     core_far[-1].wait_recv()
     add(twin_held[1, early:], 1 - core)
 
-    for copies in (far_stream, near_stream, twin_stream, core_own, core_far):
+    @pl.when(jnp.logical_not(jnp.logical_and(core == 0, second_wraps)))
+    def _():
+        for copy in far_first:
+            copy.wait_send()
+
+    for copies in (far_second, near_stream, twin_stream, core_own, core_far):
         for copy in copies:
             copy.wait_send()
 

time: 37.1 us -> 39.8 us (1.073)
  Pallas kernels: 34.8 us -> 37.4 us
    pallas_call x1, Pallas kernels: 33.6 us -> 36.2 us  [local(): pl.pallas_call(kernel, out_shape=pltpu.VMEM((2, rows, width), jnp.float32...]
where the time goes in v8:
time: 39.8 us; the launch traced here: 39.3 us
  Pallas kernels  37.4 us (94%)
  between operations  1.93 us (5%)
    pallas_call x1, Pallas kernels, local(): pl.pallas_call(kernel, out_shape=pltpu.VMEM((2, rows, width), jnp.float32...  36.2 us
    pallas_call x1, Pallas kernels, local(): pl.pallas_call(write_out, out_shape=(block, block), in_specs=[pl.BlockSpe...  1.22 us

profile of v8, /device:TPU:0, one launch (start us, length us, event | category | flops | bytes accessed | tf_op | source)
XLA Modules:
  0.0 39.3 jit_solution(9022387598845422406)
XLA Ops:
  1.9 36.2 %shard_map.59.total = f32[2,192,1152]{2,1,0:T(8,128)S(1)} custom-call(f32[1]{0:T(128)S(6)} %copy.6.log_scale_ref, f32[1]{0:T(128)S(6)} %copy.7.bias_ref, bf16[192,1152]{1,0:T(8,128)(2,1)} %image_ref.1, bf16[192,1152]{1,0:T(8,128)(2,1)} %text_ref.1), custom_call_target="tpu_custom_call" | custom-call | flops 1698693120 | bytes 2654208 | tf_op jit(solution)/shard_map/pallas_call | solution.py:226
  38.1 1.2 %shard_map.60 = (f32[192,1152]{1,0:T(8,128)}, f32[192,1152]{1,0:T(8,128)}) custom-call(f32[2,192,1152]{2,1,0:T(8,128)S(1)} %shard_map.59.total), custom_call_target="tpu_custom_call" | custom-call | bytes 3538944 | tf_op jit(solution)/shard_map/pallas_call | solution.py:247

commit v9 on v6

--- a/solution.py
+++ b/solution.py
@@ -6,8 +6,8 @@
 from jax.sharding import PartitionSpec as P
 
 SHIFTS = 4
-SIZES = (32, 64, 64, 32)
-STARTS = (0, 32, 96, 160)
+SIZES = (48, 48, 48, 48)
+STARTS = (0, 48, 96, 144)
 CHUNKS = len(SIZES)
 
 FAR_FIRST = 0
@@ -89,18 +89,12 @@
     far_first, far_second = far_stream[:CHUNKS], far_stream[CHUNKS:]
     near_own, near_far = near_stream[:CHUNKS], near_stream[CHUNKS:]
 
-    def start(*groups):
-        for group in groups:
-            for copy in group:
-                copy.start()
-
-    @pl.when(core == 0)
-    def _():
-        start(far_first, core_own, near_own)
-
-    @pl.when(core != 0)
-    def _():
-        start(near_own, core_own, far_first)
+    for i in chunks:
+        far_first[i].start()
+        near_own[i].start()
+    for i in chunks:
+        far_second[i].start()
+        core_own[i].start()
 
     scale = jnp.exp(jnp.full((1, rows), log_scale_ref[0], jnp.float32))
     offset = bias_ref[0]
@@ -134,33 +128,17 @@
         copy.wait_recv()
     add(twin_held[0], core)
 
-    def take_far(second_too):
-        for i in chunks:
-            far_first[i].wait_recv()
-            near_far[i].start()
-
-            @pl.when(side == core)
-            def _():
-                core_far[i].start()
-
-        if second_too:
-            start(far_second)
-
-    def take_near():
-        for i in chunks:
-            near_own[i].wait_recv()
-            twin_stream[i].start()
-
-    @pl.when(core == 0)
-    def _():
-        take_far(True)
-        take_near()
-
-    @pl.when(core != 0)
-    def _():
-        take_near()
-        start(far_second)
-        take_far(False)
+    for i in chunks:
+        far_first[i].wait_recv()
+        near_far[i].start()
+
+        @pl.when(side == core)
+        def _():
+            core_far[i].start()
+
+    for i in chunks:
+        near_own[i].wait_recv()
+        twin_stream[i].start()
 
     for i in chunks:
         add_batch(i)
@@ -176,13 +154,10 @@
         if i > 0:
             add_batch(CHUNKS + i - 1)
 
-    early = STARTS[-1]
-    for copy in core_far[:-1]:
+    for copy in core_far:
         copy.wait_recv()
-    add(twin_held[1, :early], 1 - core)
+    add(twin_held[1], 1 - core)
     add_batch(2 * CHUNKS - 1)
-    core_far[-1].wait_recv()
-    add(twin_held[1, early:], 1 - core)
 
     for copies in (far_stream, near_stream, twin_stream, core_own, core_far):
         for copy in copies:

time: 39 us -> 36.5 us (0.936)
  the two profiles are of different devices: /device:TPU:3 before, /device:TPU:0 now
where the time goes in v9:
time: 36.5 us; the launch traced here: 36.1 us
  Pallas kernels  34.1 us (93%)
  between operations  1.93 us (5%)
    pallas_call x1, Pallas kernels, local(): pl.pallas_call(kernel, out_shape=pltpu.VMEM((2, rows, width), jnp.float32...  32.9 us
    pallas_call x1, Pallas kernels, local(): pl.pallas_call(write_out, out_shape=(block, block), in_specs=[pl.BlockSpe...  1.22 us

profile of v9, /device:TPU:0, one launch (start us, length us, event | category | flops | bytes accessed | tf_op | source)
XLA Modules:
  0.0 36.1 jit_solution(14642260475434041756)
XLA Ops:
  1.9 32.9 %shard_map.59.total = f32[2,192,1152]{2,1,0:T(8,128)S(1)} custom-call(f32[1]{0:T(128)S(6)} %copy.6.log_scale_ref, f32[1]{0:T(128)S(6)} %copy.7.bias_ref, bf16[192,1152]{1,0:T(8,128)(2,1)} %image_ref.1, bf16[192,1152]{1,0:T(8,128)(2,1)} %text_ref.1), custom_call_target="tpu_custom_call" | custom-call | flops 1698693120 | bytes 2654208 | tf_op jit(solution)/shard_map/pallas_call | solution.py:183
  34.8 1.2 %shard_map.60 = (f32[192,1152]{1,0:T(8,128)}, f32[192,1152]{1,0:T(8,128)}) custom-call(f32[2,192,1152]{2,1,0:T(8,128)S(1)} %shard_map.59.total), custom_call_target="tpu_custom_call" | custom-call | bytes 3538944 | tf_op jit(solution)/shard_map/pallas_call | solution.py:204

commit v10 on v9

--- a/solution.py
+++ b/solution.py
@@ -93,7 +93,6 @@
         far_first[i].start()
         near_own[i].start()
     for i in chunks:
-        far_second[i].start()
         core_own[i].start()
 
     scale = jnp.exp(jnp.full((1, rows), log_scale_ref[0], jnp.float32))
@@ -127,6 +126,8 @@
     for copy in core_own:
         copy.wait_recv()
     add(twin_held[0], core)
+    for copy in far_second:
+        copy.start()
 
     for i in chunks:
         far_first[i].wait_recv()

time: 36.5 us -> 37.6 us (1.030)
  the two profiles are of different devices: /device:TPU:0 before, /device:TPU:7 now
where the time goes in v10:
time: 37.6 us; the launch traced here: 37.4 us
  Pallas kernels  35.5 us (94%)
  between operations  1.93 us (5%)
    pallas_call x1, Pallas kernels, local(): pl.pallas_call(kernel, out_shape=pltpu.VMEM((2, rows, width), jnp.float32...  34.3 us
    pallas_call x1, Pallas kernels, local(): pl.pallas_call(write_out, out_shape=(block, block), in_specs=[pl.BlockSpe...  1.22 us

profile of v10, /device:TPU:7, one launch (start us, length us, event | category | flops | bytes accessed | tf_op | source)
XLA Modules:
  0.0 37.4 jit_solution(14389846742008903634)
XLA Ops:
  1.9 34.3 %shard_map.59.total = f32[2,192,1152]{2,1,0:T(8,128)S(1)} custom-call(f32[1]{0:T(128)S(6)} %copy.6.log_scale_ref, f32[1]{0:T(128)S(6)} %copy.7.bias_ref, bf16[192,1152]{1,0:T(8,128)(2,1)} %image_ref.1, bf16[192,1152]{1,0:T(8,128)(2,1)} %text_ref.1), custom_call_target="tpu_custom_call" | custom-call | flops 1698693120 | bytes 2654208 | tf_op jit(solution)/shard_map/pallas_call | solution.py:184
  36.2 1.2 %shard_map.60 = (f32[192,1152]{1,0:T(8,128)}, f32[192,1152]{1,0:T(8,128)}) custom-call(f32[2,192,1152]{2,1,0:T(8,128)S(1)} %shard_map.59.total), custom_call_target="tpu_custom_call" | custom-call | bytes 3538944 | tf_op jit(solution)/shard_map/pallas_call | solution.py:205

commit v11 on v9

--- a/solution.py
+++ b/solution.py
@@ -6,8 +6,8 @@
 from jax.sharding import PartitionSpec as P
 
 SHIFTS = 4
-SIZES = (48, 48, 48, 48)
-STARTS = (0, 48, 96, 144)
+SIZES = (96, 96)
+STARTS = (0, 96)
 CHUNKS = len(SIZES)
 
 FAR_FIRST = 0

time: 36.5 us -> 36.3 us (level)
  the two profiles are of different devices: /device:TPU:0 before, /device:TPU:4 now
where the time goes in v11:
time: 36.3 us; the launch traced here: 36.1 us
  Pallas kernels  34.2 us (94%)
  between operations  1.93 us (5%)
    pallas_call x1, Pallas kernels, local(): pl.pallas_call(kernel, out_shape=pltpu.VMEM((2, rows, width), jnp.float32...  33 us
    pallas_call x1, Pallas kernels, local(): pl.pallas_call(write_out, out_shape=(block, block), in_specs=[pl.BlockSpe...  1.22 us

profile of v11, /device:TPU:4, one launch (start us, length us, event | category | flops | bytes accessed | tf_op | source)
XLA Modules:
  0.0 36.1 jit_solution(6715316496687418033)
XLA Ops:
  1.9 33.0 %shard_map.59.total = f32[2,192,1152]{2,1,0:T(8,128)S(1)} custom-call(f32[1]{0:T(128)S(6)} %copy.6.log_scale_ref, f32[1]{0:T(128)S(6)} %copy.7.bias_ref, bf16[192,1152]{1,0:T(8,128)(2,1)} %image_ref.1, bf16[192,1152]{1,0:T(8,128)(2,1)} %text_ref.1), custom_call_target="tpu_custom_call" | custom-call | flops 1698693120 | bytes 2654208 | tf_op jit(solution)/shard_map/pallas_call | solution.py:183
  34.9 1.2 %shard_map.60 = (f32[192,1152]{1,0:T(8,128)}, f32[192,1152]{1,0:T(8,128)}) custom-call(f32[2,192,1152]{2,1,0:T(8,128)S(1)} %shard_map.59.total), custom_call_target="tpu_custom_call" | custom-call | bytes 3538944 | tf_op jit(solution)/shard_map/pallas_call | solution.py:204
